TPU v7x, 32 devices: a whole 2x2x4 slice. The times are simulated.
32 devices in a mesh: dp: 8 (over z, x), head: 4 (over y, core).
Axes of the slice: x: 2, y: 2, z: 4, core: 2. Of those that a mesh axis runs over, the one named last changes fastest.
Arguments:
- token_ids: int32 [2, 4096], P(None, ('dp', 'head')), may hold values from 0 to 31999
- lengths: int32 [2, 8, 3], P(None, 'dp'), may hold values from 1 to 409, 512 in all within a row
- valid: int32 [2, 4096], P(None, ('dp', 'head')), may hold values 0 or 1
- vocab_ids: int32 [4096], replicated, may hold values from 0 to 31999, as said below
- teacher: bfloat16 [2, 4096, 4096], P(None, ('dp', 'head')), may hold values from -12 to 12
- block: float32 [768, 12288], P(None, ('dp', 'head'))
- block_m: float32 [768, 12288], P(None, ('dp', 'head')), may hold values from -2.3841858e-07 to 2.3841858e-07
- block_v: float32 [768, 12288], P(None, ('dp', 'head')), may hold values from 1.1876942e-15 to 4.750777e-15
- bases: float32 [4, 768, 768], replicated
- table: float32 [32000, 768], P('dp'), may hold values from -0.4375 to 0.4375
- table_m: float32 [32000, 768], P('dp'), may hold values from -2.3841858e-07 to 2.3841858e-07
- table_v: float32 [32000, 768], P('dp'), may hold values from 1.1876942e-15 to 4.750777e-15
- gains: float32 [3, 768], replicated, may hold values from 0.5 to 1.5
- gains_m: float32 [3, 768], replicated, may hold values from -9.536743e-07 to 9.536743e-07
- gains_v: float32 [3, 768], replicated, may hold values from 1.899135e-14 to 7.6141784e-14
Outputs:
- loss: float32 [], replicated
- grad_norm: float32 [], replicated
- block_new: float32 [768, 12288], P(None, ('dp', 'head'))
- block_m_new: float32 [768, 12288], P(None, ('dp', 'head'))
- block_v_new: float32 [768, 12288], P(None, ('dp', 'head'))
- table_new: float32 [32000, 768], P('dp')
- table_m_new: float32 [32000, 768], P('dp')
- table_v_new: float32 [32000, 768], P('dp')
- gains_new: float32 [3, 768], replicated
- gains_m_new: float32 [3, 768], replicated
- gains_v_new: float32 [3, 768], replicated
- block_low: bfloat16 [768, 12288], P(None, ('dp', 'head'))
- table_low: bfloat16 [32000, 768], P('dp')
Inputs may be any that keep to these rules, and one draw needn't show every extreme that they name: `vocab_ids`: distinct ids. Each row holds the lengths of 3 sequences packed in order into one bucket; they sum to 512 and the largest is exactly 409.
All inputs are finite; a program needn't handle non-finite values. No bound on the sum of `valid` on one device may be relied on, other than what follows from the above.
Results may differ from a plain program's by a relative error of at most 0.02.
Values may be sent and summed in bfloat16 or wider, within the bound.
A program may use at most 248 MiB of HBM per device.

v0:
```python
import math
import jax
import jax.numpy as jnp
from jax import lax
from jax.sharding import PartitionSpec as P

D = 768
H = 12
HD = 64
FF = 3072
TOPV = 4096
STEP = 5
low = jnp.bfloat16
scale = HD ** (-0.5)
eps_norm = 1e-05
clip_norm = 0.002
beta_one = 0.9
beta_two = 0.99
adam_eps = 1e-08
decay_rate = 0.1
rate_block = 0.03
rate_table = 0.05
rate_gain = 0.4


def product(left, right):
    return jnp.dot(left, right, preferred_element_type=jnp.float32)


def contract_rows(left, right):
    return lax.dot_general(
        left, right, (((0,), (0,)), ((), ())), preferred_element_type=jnp.float32
    )


def contract_cols(left, right):
    return lax.dot_general(
        left, right, (((1,), (1,)), ((), ())), preferred_element_type=jnp.float32
    )


def rms_norm(value, gain):
    return value * lax.rsqrt(jnp.mean(value * value, axis=-1, keepdims=True) + eps_norm) * gain


def rms_back(value, gain, grad):
    r = lax.rsqrt(jnp.mean(value * value, axis=-1, keepdims=True) + eps_norm)
    scaled = grad * gain
    d_value = r * scaled - value * (r * r * r) * jnp.mean(value * scaled, axis=-1, keepdims=True)
    return (d_value, jnp.sum(grad * value * r, axis=0))


def rotary(value, cosine, sine):
    half = HD // 2
    turned = jnp.concatenate([-value[..., half:], value[..., :half]], axis=-1)
    return value * cosine[:, None, :] + turned * sine[:, None, :]


def rotary_back(grad, cosine, sine):
    half = HD // 2
    part = grad * sine[:, None, :]
    turned = jnp.concatenate([part[..., half:], -part[..., :half]], axis=-1)
    return grad * cosine[:, None, :] + turned


def segments(lengths, places):
    segment = jnp.zeros_like(places)
    begin = jnp.zeros_like(places)
    end = jnp.zeros((), jnp.int32)
    for index in range(lengths.shape[0] - 1):
        end = end + lengths[index]
        past = places >= end
        segment = segment + past.astype(jnp.int32)
        begin = jnp.where(past, end, begin)
    return (segment, places - begin)


def scores_of(query, keys, allow):
    score = jnp.einsum("qhd,khd->hqk", query, keys, preferred_element_type=jnp.float32) * scale
    return jnp.where(allow[None], score, -1e30)


def attend(query, keys, values, allow):
    score = scores_of(query, keys, allow)
    summit = jnp.max(score, axis=-1, keepdims=True)
    log_total = summit + jnp.log(jnp.sum(jnp.exp(score - summit), axis=-1, keepdims=True))
    weight = jnp.exp(score - log_total)
    mixed = jnp.einsum(
        "hqk,khd->qhd", weight.astype(low), values, preferred_element_type=jnp.float32
    )
    return (mixed.astype(low), log_total)


def attend_back(query, keys, values, log_total, upstream, allow):
    weight = jnp.exp(scores_of(query, keys, allow) - log_total)
    d_value = jnp.einsum(
        "hqk,qhd->khd", weight.astype(low), upstream, preferred_element_type=jnp.float32
    )
    d_weight = jnp.einsum("qhd,khd->hqk", upstream, values, preferred_element_type=jnp.float32)
    d_score = (weight * (d_weight - jnp.sum(d_weight * weight, axis=-1, keepdims=True))).astype(low)
    d_query = jnp.einsum("hqk,khd->qhd", d_score, keys, preferred_element_type=jnp.float32) * scale
    d_key = jnp.einsum("hqk,qhd->khd", d_score, query, preferred_element_type=jnp.float32) * scale
    return (d_query, d_key, d_value)


def swap(value, head_count, offset):
    return lax.ppermute(value, "head", [(h, h ^ offset) for h in range(head_count)])


def layer_forward(hidden, weights, gains, cosine, sine, allow, head_count):
    w_qkv, w_out, w_gu, w_down = weights
    rows = hidden.shape[0]
    normed = rms_norm(hidden, gains[0]).astype(low)
    qkv = contract_cols(normed, w_qkv).reshape(rows, 3, H, HD)
    query = rotary(qkv[:, 0], cosine, sine).astype(low)
    key = rotary(qkv[:, 1], cosine, sine).astype(low)
    own = jnp.concatenate([key, qkv[:, 2].astype(low)], axis=1)
    both = jnp.concatenate([own, swap(own, head_count, 1)], axis=0)
    keys, values = (both[:, :H], both[:, H:])
    mixed, log_total = attend(query, keys, values, allow)
    merged = mixed.reshape(rows, D)
    middle = hidden + contract_cols(merged, w_out)
    normed_two = rms_norm(middle, gains[1]).astype(low)
    gate_up = contract_cols(normed_two, w_gu)
    action = (jax.nn.silu(gate_up[:, :FF]) * gate_up[:, FF:]).astype(low)
    output = middle + product(action, w_down)
    saved = (
        hidden,
        normed,
        query,
        keys,
        values,
        log_total,
        merged,
        middle,
        normed_two,
        gate_up,
        action,
    )
    return (output, saved)


def layer_backward(gradient, weights, gains, saved, cosine, sine, allow, head_count):
    w_qkv, w_out, w_gu, w_down = weights
    hidden, normed, query, keys, values, log_total, merged, middle, normed_two, gate_up, action = (
        saved
    )
    rows = hidden.shape[0]
    grad_low = gradient.astype(low)
    d_down = contract_rows(action, grad_low)
    d_action = contract_cols(grad_low, w_down)
    gate, up = (gate_up[:, :FF], gate_up[:, FF:])
    chance = jax.nn.sigmoid(gate)
    d_gate = d_action * up * (chance + gate * chance * (1.0 - chance))
    d_up = d_action * gate * chance
    d_gate_up = jnp.concatenate([d_gate, d_up], axis=1).astype(low)
    d_gu = contract_rows(d_gate_up, normed_two)
    d_middle, d_gain_two = rms_back(middle, gains[1], product(d_gate_up, w_gu))
    d_middle = gradient + d_middle
    middle_low = d_middle.astype(low)
    d_out = contract_rows(middle_low, merged)
    upstream = product(middle_low, w_out).astype(low).reshape(rows, H, HD)
    d_query, d_key, d_value = attend_back(query, keys, values, log_total, upstream, allow)
    d_own = jnp.concatenate([d_key[:rows], d_value[:rows]], axis=1)
    d_far = jnp.concatenate([d_key[rows:], d_value[rows:]], axis=1).astype(low)
    d_own = (d_own + swap(d_far, head_count, 1).astype(jnp.float32)).astype(low).astype(jnp.float32)
    d_query = rotary_back(d_query.astype(low).astype(jnp.float32), cosine, sine)
    d_key = rotary_back(d_own[:, :H], cosine, sine)
    d_qkv = jnp.concatenate([d_query, d_key, d_own[:, H:]], axis=1).reshape(rows, 3 * D).astype(low)
    d_qkv_w = contract_rows(d_qkv, normed)
    d_hidden, d_gain_one = rms_back(hidden, gains[0], product(d_qkv, w_qkv))
    return (d_middle + d_hidden, [d_qkv_w, d_out, d_gu, d_down], d_gain_one, d_gain_two)


def adam_step(weight, gradient, first, second, rate, decay):
    first_new = beta_one * first + (1.0 - beta_one) * gradient
    second_new = beta_two * second + (1.0 - beta_two) * gradient * gradient
    direction = (
        first_new
        / (1.0 - beta_one**STEP)
        / (jnp.sqrt(second_new / (1.0 - beta_two**STEP)) + adam_eps)
    )
    return (weight - rate * (direction + decay * weight), first_new, second_new)


def on_device(
    token_ids,
    lengths,
    valid,
    vocab_ids,
    teacher,
    block,
    block_m,
    block_v,
    bases,
    table,
    table_m,
    table_v,
    gains,
    gains_m,
    gains_v,
):
    dp_count, head_count = (lax.axis_size("dp"), lax.axis_size("head"))
    device_total = dp_count * head_count
    head, dp = (lax.axis_index("head"), lax.axis_index("dp"))
    batch = head // 2
    tokens = token_ids.shape[1]
    shard_rows = table.shape[0]
    offset = dp * shard_rows
    part = TOPV // device_total
    codes = lax.all_gather(token_ids * 2 + valid, ("dp", "head"), axis=1, tiled=True)
    count = jnp.sum(codes & 1).astype(jnp.float32)
    codes = lax.dynamic_index_in_dim(codes, batch, 0, keepdims=False).reshape(
        dp_count, head_count, tokens
    )
    first = lax.dynamic_index_in_dim(codes, head, 1, keepdims=False)
    second = lax.dynamic_index_in_dim(codes, head ^ 2, 1, keepdims=False)
    codes = jnp.concatenate([first, second], axis=1)
    weighting = (lax.dynamic_index_in_dim(codes, dp, 0, keepdims=False) & 1).astype(jnp.float32)
    vocab = lax.dynamic_index_in_dim(
        vocab_ids.reshape(dp_count, head_count, part), head, 1, keepdims=False
    )
    local = jnp.concatenate([vocab, codes >> 1], axis=1) - offset
    owned = (local >= 0) & (local < shard_rows)
    rows_out = jnp.where(owned[..., None], table[jnp.clip(local, 0, shard_rows - 1)], 0.0).astype(
        low
    )
    rows_in = lax.psum_scatter(rows_out, "dp", scatter_dimension=0, tiled=True)
    rows_in = rows_in.reshape(part + 2 * tokens, D)
    chosen = lax.all_gather(rows_in[:part], ("dp", "head"), axis=0, tiled=True)
    hidden = rows_in[part:].astype(jnp.float32)
    widths = [3 * D // device_total, D // device_total, 2 * FF // device_total, FF // device_total]
    cuts = [sum(widths[:index]) for index in range(5)]
    gathered = lax.all_gather(block.T.astype(low), ("dp", "head"), axis=0)
    weights = [gathered[:, cuts[index] : cuts[index + 1]].reshape(-1, D) for index in range(4)]
    teacher_own = lax.dynamic_index_in_dim(teacher, batch, 0, keepdims=False)
    teacher_far = swap(
        lax.dynamic_index_in_dim(teacher, 1 - batch, 0, keepdims=False), head_count, 2
    )
    teacher_rows = jnp.concatenate([teacher_own, teacher_far], axis=0)
    run = jnp.arange(tokens, dtype=jnp.int32)
    places = jnp.concatenate([head * tokens + run, (head ^ 2) * tokens + run])
    places_far = jnp.concatenate([(head ^ 1) * tokens + run, (head ^ 3) * tokens + run])
    own_lengths = lax.dynamic_index_in_dim(lengths, batch, 0, keepdims=False)[0]
    segment, position = segments(own_lengths, places)
    segment_far, unused = segments(own_lengths, places_far)
    places_all = jnp.concatenate([places, places_far])
    segment_all = jnp.concatenate([segment, segment_far])
    allow = (segment[:, None] == segment_all[None, :]) & (places[:, None] >= places_all[None, :])
    freqs = jnp.exp(jnp.arange(0, HD, 2, dtype=jnp.float32) * (-math.log(10000.0) / HD))
    angle = position.astype(jnp.float32)[:, None] * freqs[None, :]
    angle = jnp.concatenate([angle, angle], axis=1)
    cosine, sine = (jnp.cos(angle), jnp.sin(angle))
    saves = []
    for repeat in range(2):
        hidden, saved = layer_forward(hidden, weights, gains, cosine, sine, allow, head_count)
        saves.append(saved)
    normed = rms_norm(hidden, gains[2]).astype(low)
    log_prob = jax.nn.log_softmax(contract_cols(normed, chosen), axis=-1)
    teach = jax.nn.log_softmax(teacher_rows.astype(jnp.float32), axis=-1)
    loss_sum = jnp.sum(weighting * jnp.sum(jnp.exp(teach) * (teach - log_prob), axis=-1))
    logit_grads = ((jnp.exp(log_prob) - jnp.exp(teach)) * weighting[:, None]).astype(low)
    chosen_grads = contract_rows(logit_grads, normed).astype(low)
    gradient, d_gain_final = rms_back(hidden, gains[2], product(logit_grads, chosen))
    chosen_grads = lax.psum_scatter(chosen_grads, ("dp", "head"), scatter_dimension=0, tiled=True)
    block_grads = None
    d_gains = [0.0, 0.0]
    for repeat in range(2):
        gradient, layer_grads, d_gain_one, d_gain_two = layer_backward(
            gradient, weights, gains, saves[1 - repeat], cosine, sine, allow, head_count
        )
        d_gains = [d_gains[0] + d_gain_one, d_gains[1] + d_gain_two]
        if block_grads is None:
            block_grads = layer_grads
        else:
            block_grads = [total + extra for total, extra in zip(block_grads, layer_grads)]
    joined = jnp.concatenate(
        [piece.astype(low).reshape(device_total, -1, D) for piece in block_grads], axis=1
    )
    block_grads = lax.psum_scatter(joined, ("dp", "head"), scatter_dimension=0, tiled=True)
    block_grads = block_grads.reshape(-1, D).astype(jnp.float32).T
    rows_back = jnp.concatenate([chosen_grads, gradient.astype(low)], axis=0)
    rows_back = lax.all_gather(rows_back, "dp", axis=0, tiled=True)
    dump_index = jnp.where(owned, local, shard_rows).reshape(-1)
    table_grads = jax.ops.segment_sum(
        rows_back.astype(jnp.float32), dump_index, num_segments=shard_rows + 1
    )[:shard_rows]
    table_grads = lax.psum(table_grads.astype(low), "head").astype(jnp.float32)
    small = jnp.concatenate([d_gains[0], d_gains[1], d_gain_final, loss_sum[None]])
    small = lax.psum(small, ("dp", "head"))
    gain_grads = small[: 3 * D].reshape(3, D) / count
    loss = small[3 * D] / count
    squares = lax.psum(
        jnp.sum(block_grads * block_grads)
        + jnp.where(head == 0, jnp.sum(table_grads * table_grads), 0.0),
        ("dp", "head"),
    )
    grad_norm = jnp.sqrt(squares / (count * count) + jnp.sum(gain_grads * gain_grads))
    clip = jnp.minimum(1.0, clip_norm / grad_norm)
    factor = clip / count
    block_grads = block_grads * factor
    table_grads = table_grads * factor
    gain_grads = gain_grads * clip
    rotated = jnp.concatenate(
        [
            contract_rows(bases[index], block_grads[:, cuts[index] : cuts[index + 1]])
            for index in range(4)
        ],
        axis=1,
    )
    block_m_new = beta_one * block_m + (1.0 - beta_one) * rotated
    block_v_new = beta_two * block_v + (1.0 - beta_two) * rotated * rotated
    direction = (
        block_m_new
        / (1.0 - beta_one**STEP)
        / (jnp.sqrt(block_v_new / (1.0 - beta_two**STEP)) + adam_eps)
    )
    update = jnp.concatenate(
        [product(bases[index], direction[:, cuts[index] : cuts[index + 1]]) for index in range(4)],
        axis=1,
    )
    block_new = block - rate_block * (update + decay_rate * block)
    table_new, table_m_new, table_v_new = adam_step(
        table, table_grads, table_m, table_v, rate_table, decay_rate
    )
    gains_new, gains_m_new, gains_v_new = adam_step(
        gains, gain_grads, gains_m, gains_v, rate_gain, 0.0
    )
    return (
        loss,
        grad_norm,
        block_new,
        block_m_new,
        block_v_new,
        table_new,
        table_m_new,
        table_v_new,
        gains_new,
        gains_m_new,
        gains_v_new,
        block_new.astype(low),
        table_new.astype(low),
    )


def solution(mesh):
    tokens = P(None, ("dp", "head"))
    columns = P(None, ("dp", "head"))
    table = P("dp", None)
    return jax.shard_map(
        on_device,
        mesh=mesh,
        in_specs=(
            tokens,
            P(None, "dp", None),
            tokens,
            P(),
            P(None, ("dp", "head"), None),
            columns,
            columns,
            columns,
            P(),
            table,
            table,
            table,
            P(),
            P(),
            P(),
        ),
        out_specs=(
            P(),
            P(),
            columns,
            columns,
            columns,
            table,
            table,
            table,
            P(),
            P(),
            P(),
            columns,
            table,
        ),
        check_vma=False,
    )
```

profile of v0, /device:TPU:0, one launch (start us, length us, event | category | flops | bytes accessed | tf_op | source)
XLA Modules:
  0.0 969.5 jit_solution(10707794897695880077)
XLA Ops:
  8.8 43.2 %all_gather.15 = s32[2,4096]{1,0:T(2,128)S(1)} all-gather(s32[2,128]{1,0:T(2,128)S(1)} %multiply_add_fusion.2), channel_id=1, replica_groups=mesh['dp'=8,'head'=4] {'dp','head'}, dimensions={1}, use_global_device_ids=true | all-gather | bytes 33792 | tf_op jit(solution)/shard_map/all_gather | solution.py:211
  53.4 19.0 %gather_fusion = bf16[3072,768]{1,0:T(8,128)(2,1)} fusion(f32[4000,768]{1,0:T(8,128)} %param.25, s32[3072]{0:T(1024)S(1)} %broadcast_clamp_fusion), kind=kCustom, calls=%fused_computation | custom fusion | bytes 9449472 | tf_op jit(solution)/shard_map/gather | solution.py:225
  72.5 5.8 select_convert_fusion
  85.2 155.6 %reduce-scatter.4.cloned.1.call-done = bf16[1,384,768]{2,1,0:T(8,128)(2,1)} async-done(((bf16[8,384,768]{2,1,0:T(8,128)(2,1)}), bf16[1,384,768]{2,1,0:T(8,128)(2,1)}) %reduce-scatter.4.cloned.1.call-update) | async-done | bytes 589840 | tf_op jit(solution)/shard_map/reduce_scatter | solution.py:228
  242.5 24.5 %copy.41 = bf16[12288,768]{1,0:T(8,128)(2,1)} copy(bf16[12288,768]{0,1:T(8,128)(2,1)} %all-gather.8.cloned.1.call-done) | data formatting | bytes 37748736 | tf_op jit(solution)/shard_map/all_gather | solution.py:234
  283.6 8.4 slice.321
  292.0 4.9 slice.324
  312.5 4.4 multiply_reduce_fusion.12
  342.8 5.2 multiply_reduce_fusion.10
  350.0 5.0 fusion.192
  373.4 4.6 convolution_bitcast_fusion.1
  386.3 4.7 convolution_convert_fusion
  432.5 71.6 %reduce-scatter.8.cloned.1.call-done = bf16[128,768]{1,0:T(8,128)(2,1)} async-done(((bf16[4096,768]{1,0:T(8,128)(2,1)}), bf16[128,768]{1,0:T(8,128)(2,1)}) %reduce-scatter.8.cloned.1.call-update) | async-done | bytes 196624 | tf_op jit(solution)/shard_map/reduce_scatter | solution.py:265
  510.6 8.2 fusion.50
  524.5 11.0 %add_convert_fusion = bf16[6144,768]{1,0:T(8,128)(2,1)} fusion(f32[6144,768]{1,0:T(8,128)} %fusion.50, bf16[256,3072]{1,0:T(8,128)(2,1)} %copy-done.91, bf16[256,3072]{1,0:T(8,128)(2,1)S(1)} %copy-done.90, f32[256,768]{1,0:T(8,128)S(1)} %copy-done.14, f32[768]{0:T(1024)S(1)} %get-tuple-element.51, f32[256]{0:T(256)S(1)} %copy-done.112), kind=kOutput, calls=%fused_computation.3 | convolution fusion | flops 2432237568 | bytes 32247808 | tf_op jit(solution)/shard_map/dot_general | solution.py:31
  535.5 49.3 %all-gather.6.cloned.1.call-done = bf16[3072,768]{1,0:T(8,128)(2,1)} async-done(((bf16[384,768]{1,0:T(8,128)(2,1)}), bf16[3072,768]{1,0:T(8,128)(2,1)}) %all-gather.6.cloned.1.call-update) | async-done | bytes 4718608 | tf_op jit(solution)/shard_map/all_gather | solution.py:283
  584.9 26.8 %scatter_custom_fusion = f32[4001,768]{1,0:T(8,128)} fusion(s32[3072]{0:T(1024)S(1)} %bitcast.297, bf16[3072,768]{1,0:T(8,128)(2,1)} %all-gather.6.cloned.1.call-done, f32[]{:T(128)} %constant.61.clone.1), kind=kCustom, calls=%fused_computation.13 | custom fusion | flops 4718592 | bytes 17009668 | tf_op jit(solution)/shard_map/scatter-add | solution.py:285
  611.7 7.7 slice.532
  623.8 15.2 %pad_maximum_fusion = bf16[32,384,768]{2,1,0:T(8,128)(2,1)} fusion(bf16[32,96,768]{2,1,0:T(8,128)(2,1)} %bitcast.265, bf16[32,192,768]{2,1,0:T(8,128)(2,1)} %bitcast.245, bf16[32,24,768]{2,1,0:T(8,128)(2,1)S(1)} %bitcast.271, bf16[32,72,768]{2,1,0:T(8,128)(2,1)S(1)} %bitcast.266), kind=kLoop, calls=%fused_computation.2 | loop fusion | flops 75497472 | bytes 37748736 | tf_op jit(solution)/shard_map/concatenate | solution.py:277
  646.5 97.7 %all-reduce.3.cloned.1.call-done = bf16[4000,768]{1,0:T(8,128)(2,1)} async-done(((bf16[4000,768]{1,0:T(8,128)(2,1)}), bf16[4000,768]{1,0:T(8,128)(2,1)}) %all-reduce.3.cloned.1.call-update) | async-done | bytes 6144016 | tf_op jit(solution)/shard_map/psum | solution.py:288
  744.2 6.6 fusion.2
  751.5 106.8 %reduce-scatter.6.cloned.1.call-done = bf16[1,384,768]{2,1,0:T(8,128)(2,1)} async-done(((bf16[32,384,768]{2,1,0:T(8,128)(2,1)}), bf16[1,384,768]{2,1,0:T(8,128)(2,1)}) %reduce-scatter.6.cloned.1.call-update) | async-done | bytes 589840 | tf_op jit(solution)/shard_map/reduce_scatter | solution.py:280
  860.9 39.9 %all-reduce = (f32[2305]{0:T(1024)S(1)}, f32[]{:T(128)}) all-reduce(f32[2305]{0:T(1024)S(1)} %pad_maximum_fusion.18, f32[]{:T(128)S(6)} %add.365), channel_id=1, replica_groups=mesh['dp'=8,'head'=4] {'dp','head'}, use_global_device_ids=true, to_apply=%region_25.27 | all-reduce | flops 2306 | bytes 18448 | tf_op jit(solution)/shard_map/psum | solution.py:290
  930.8 28.9 %fusion.180 = (bf16[4000,768]{1,0:T(8,128)(2,1)}, f32[4000,768]{1,0:T(8,128)}, f32[4000,768]{1,0:T(8,128)}, f32[4000,768]{1,0:T(8,128)}) fusion(f32[4000,768]{1,0:T(8,128)} %param.25, f32[]{:T(128)S(6)} %div.137, bf16[4000,768]{1,0:T(8,128)(2,1)} %all-reduce.3.cloned.1.call-done, f32[4000,768]{1,0:T(8,128)} %param.26, f32[4000,768]{1,0:T(8,128)} %param.27), kind=kLoop, calls=%fused_computation.347 | loop fusion | flops 55296000 | bytes 86016000 | tf_op jit(solution)/shard_map/convert_element_type | solution.py:342
  (528 shorter events, 188.8 us)
Async XLA Ops:
  8.0 72.6 %copy-start = (s32[2,1,3]{2,1,0:T(1,128)S(1)}, s32[2,1,3]{2,1,0:T(1,128)}, u32[]{:S(2)}) copy-start(s32[2,1,3]{2,1,0:T(1,128)} %param.17) | copy-start | bytes 76
  8.0 232.8 %reduce-scatter.4.cloned.1.call-start = ((), (), s32[]{:S(2)}) async-start(), calls=%async_computation.3 | async-start | bytes 5308416 | tf_op jit(solution)/shard_map/reduce_scatter | solution.py:228
  52.0 20.4 %copy-start.95 = (s32[2,4096]{1,0:T(2,128)}, s32[2,4096]{1,0:T(2,128)S(1)}, u32[]{:S(2)}) copy-start(s32[2,4096]{1,0:T(2,128)S(1)} %all_gather.15) | copy-start | bytes 98308
  52.8 19.7 %copy-start.103 = (s32[8,1,128]{2,1,0:T(1,128)}, s32[8,1,128]{2,1,0:T(1,128)S(1)}, u32[]{:S(2)}) copy-start(s32[8,1,128]{2,1,0:T(1,128)S(1)} %get-tuple-element.156) | copy-start | bytes 12292
  78.4 164.2 %all-gather.8.cloned.1.call-start = ((), (), s32[]{:S(2)}) async-start(), calls=%async_computation.8 | async-start | bytes 19464192 | tf_op jit(solution)/shard_map/all_gather | solution.py:234
  80.5 269.5 %all-gather.10.cloned.1.call-start = ((), (), s32[]{:S(2)}) async-start(), calls=%async_computation.9 | async-start | bytes 6488064 | tf_op jit(solution)/shard_map/all_gather | solution.py:230
  83.1 184.0 %copy-start.136 = (s32[128]{0:T(128)}, s32[128]{0:T(128)S(1)}, u32[]{:S(2)}) copy-start(s32[128]{0:T(128)S(1)} %iota_add_fusion.3) | copy-start | bytes 1540
  269.4 48.3 %copy-start.4 = (bf16[32,72,768]{2,1,0:T(8,128)(2,1)}, bf16[32,72,768]{2,1,0:T(8,128)(2,1)S(1)}, u32[]{:S(2)}) copy-start(bf16[32,72,768]{2,1,0:T(8,128)(2,1)S(1)} %slice.311) | copy-start | bytes 10616836
  273.6 23.3 %collective-permute-start = (bf16[256,24,64]{0,2,1:T(8,128)(2,1)}, bf16[256,24,64]{0,2,1:T(8,128)(2,1)}, u32[]{:S(2)}, u32[]{:S(2)}) collective-permute-start(bf16[256,24,64]{0,2,1:T(8,128)(2,1)} %pad_maximum_fusion.12), channel_id=1, source_target_pairs={{0,1},{1,0},{2,3},{3,2},{4,5},{5,4},{6,7},{7,6},{8,9},{9,8},{10,11... | collective-permute-start | bytes 2359304 | tf_op jit(solution)/shard_map/ppermute | solution.py:107
  275.2 47.4 %collective-permute-start.2 = (bf16[128,4096]{1,0:T(8,128)(2,1)}, bf16[128,4096]{1,0:T(8,128)(2,1)}, u32[]{:S(2)}, u32[]{:S(2)}) collective-permute-start(bf16[128,4096]{1,0:T(8,128)(2,1)} %get-tuple-element.82), channel_id=1, source_target_pairs={{0,2},{1,3},{2,0},{3,1},{4,6},{5,7},{6,4},{7,5},{8,10},{9,11},{10,... | collective-permute-start | bytes 3145736 | tf_op jit(solution)/shard_map/ppermute | solution.py:107
  281.2 222.9 %reduce-scatter.8.cloned.1.call-start = ((), (), s32[]{:S(2)}) async-start(), calls=%async_computation.5 | async-start | bytes 6488064 | tf_op jit(solution)/shard_map/reduce_scatter | solution.py:265
  321.2 5.8 collective-permute-start.1
  337.3 31.7 %copy-start.15 = (f32[256,768]{1,0:T(8,128)}, f32[256,768]{1,0:T(8,128)S(1)}, u32[]{:S(2)}) copy-start(f32[256,768]{1,0:T(8,128)S(1)} %get-tuple-element.138) | copy-start | bytes 2359300
  337.4 31.6 %copy-start.108 = (f32[256]{0:T(256)}, f32[256]{0:T(256)S(1)}, u32[]{:S(2)}) copy-start(f32[256]{0:T(256)S(1)} %get-tuple-element.121) | copy-start | bytes 3076
  384.3 6.8 collective-permute-start.3
  391.0 193.8 %all-gather.6.cloned.1.call-start = ((), (), s32[]{:S(2)}) async-start(), calls=%async_computation.6 | async-start | bytes 5308416 | tf_op jit(solution)/shard_map/all_gather | solution.py:283
  422.7 2.4 collective-permute-start.4
  432.2 73.9 %copy-start.102 = (s32[8,256]{1,0:T(8,128)S(1)}, s32[8,256]{1,0:T(8,128)}, u32[]{:S(2)}) copy-start(s32[8,256]{1,0:T(8,128)} %copy-done.101) | copy-start | bytes 24580
  432.2 74.7 %copy-start.25 = (f32[256,768]{1,0:T(8,128)S(1)}, f32[256,768]{1,0:T(8,128)}, u32[]{:S(2)}) copy-start(f32[256,768]{1,0:T(8,128)} %copy-done.23) | copy-start | bytes 2359300
  432.5 76.0 %copy-start.33 = (bf16[256,3072]{1,0:T(8,128)(2,1)S(1)}, bf16[256,3072]{1,0:T(8,128)(2,1)}, u32[]{:S(2)}) copy-start(bf16[256,3072]{1,0:T(8,128)(2,1)} %copy-done.32) | copy-start | bytes 4718596
  505.9 238.4 %all-reduce.3.cloned.1.call-start = ((), (), s32[]{:S(2)}) async-start(), calls=%async_computation.7 | async-start | bytes 12288000 | tf_op jit(solution)/shard_map/psum | solution.py:288
  619.5 238.8 %reduce-scatter.6.cloned.1.call-start = ((), (), s32[]{:S(2)}) async-start(), calls=%async_computation.4 | async-start | bytes 19464192 | tf_op jit(solution)/shard_map/reduce_scatter | solution.py:280
  744.2 170.9 %slice-start.16 = ((s8[9437184]{0:T(1024)(128)(4,1)}), s8[1048576]{0:T(1024)(128)(4,1)S(1)}, s32[]{:S(2)}) async-start(s8[9437184]{0:T(1024)(128)(4,1)} %bitcast.254), calls=%async_computation.26 | async-start | bytes 2097152
  930.8 28.9 %copy-start.1 = (s32[2,1,3]{2,1,0:T(1,128)S(1)}, s32[2,1,3]{2,1,0:T(1,128)}, u32[]{:S(2)}) copy-start(s32[2,1,3]{2,1,0:T(1,128)} %param.17) | copy-start | bytes 76
  (154 other events, 588.1 us)
Sparse Core Ops, SparseCore 0:
  78.5 162.2 reduce-scatter.3
  506.0 78.8 all-gather.5
  619.6 124.5 all-reduce.2
Sparse Core Ops, SparseCore 1:
  82.3 157.9 all-gather.7
  281.3 68.7 all-gather.9
  391.1 112.9 reduce-scatter.7
  639.1 219.1 reduce-scatter.5
where the time goes:
time: 978 us; the launch traced here: 970 us
  waiting for transfers between devices  485 us (50%)
  other arithmetic  139 us (14%)
  matrix products  121 us (12%)
  local copies, waits for them, and re-layouts  113 us (12%)
  blocking collectives  83.2 us (9%)
  between operations  25.5 us (3%)
    reduce_scatter x1, waiting for transfers between devices, on_device(): rows_in = lax.psum_scatter(rows_out, 'dp', scatter_dimension=0, tiled=True)  156 us
    reduce_scatter x1, waiting for transfers between devices, on_device(): lax.psum_scatter(joined, ('dp', 'head'), scatter_dimension=0, tiled=True)  107 us
    psum x1, waiting for transfers between devices, on_device(): table_grads = lax.psum(table_grads.astype(low), 'head').astype(jnp.float32)  97.7 us
    reduce_scatter x1, waiting for transfers between devices, on_device(): lax.psum_scatter(chosen_grads, ('dp', 'head'), scatter_dimension=0, tiled...  71.6 us
    all_gather x1, waiting for transfers between devices, on_device(): rows_back = lax.all_gather(rows_back, 'dp', axis=0, tiled=True)  49.3 us
    all_gather x1, blocking collectives, on_device(): lax.all_gather(token_ids * 2 + valid, ('dp', 'head'), axis=1, tiled=True)  43.2 us
    dot_general x13, matrix products, contract_rows(): lax.dot_general(left, right, (((0,), (0,)), ((), ())), preferred_element_...  42.8 us
    psum x1, blocking collectives, on_device(): small = lax.psum(small, ('dp', 'head'))  39.9 us
  transfers between devices with their start and end apart: 12, of which 7 were waited for; matrix products, arithmetic and copies ran while one was open for 17% of the time, Pallas kernels for 0%

commit v1 on v0

--- a/solution.py
+++ b/solution.py
@@ -21,6 +21,11 @@
 rate_block = 0.03
 rate_table = 0.05
 rate_gain = 0.4
+
+
+def summed_here(block, axis):
+    parts = lax.all_gather(block, axis)
+    return jnp.sum(parts, axis=0)
 
 
 def product(left, right):
@@ -285,7 +290,7 @@
     table_grads = jax.ops.segment_sum(
         rows_back.astype(jnp.float32), dump_index, num_segments=shard_rows + 1
     )[:shard_rows]
-    table_grads = lax.psum(table_grads.astype(low), "head").astype(jnp.float32)
+    table_grads = summed_here(table_grads.astype(low), "head").astype(jnp.float32)
     small = jnp.concatenate([d_gains[0], d_gains[1], d_gain_final, loss_sum[None]])
     small = lax.psum(small, ("dp", "head"))
     gain_grads = small[: 3 * D].reshape(3, D) / count

time: 978 us -> 1030 us (1.053)
  waiting for transfers between devices: 485 us -> 509 us
  other arithmetic: 139 us -> 155 us
    reduce_scatter x1, waiting for transfers between devices: 107 us -> 254 us  [on_device(): lax.psum_scatter(joined, ('dp', 'head'), scatter_dimension=0, tiled=True)]
    psum x1 -> x0, waiting for transfers between devices: 97.7 us -> none  [on_device(): table_grads = lax.psum(table_grads.astype(low), 'head').astype(jnp.float32)]
    all_gather x1, waiting for transfers between devices: 49.3 us -> 23.2 us  [on_device(): rows_back = lax.all_gather(rows_back, 'dp', axis=0, tiled=True)]
    reduce_sum x0 -> x1, other arithmetic: none -> 17.3 us  [summed_here(): return jnp.sum(parts, axis=0)]
    unnamed x338 -> x336, local copies, waits for them, and re-layouts: 31.5 us -> 30.1 us
  transfers between devices with their start and end apart: 12 -> 12, of which waited for: 7 -> 6; matrix products, arithmetic and copies ran while one was open for 17% -> 20% of each run, Pallas kernels for 0% -> 0%
where the time goes in v1:
time: 1030 us; the launch traced here: 1020 us
  waiting for transfers between devices  509 us (49%)
  other arithmetic  155 us (15%)
  matrix products  130 us (13%)
  local copies, waits for them, and re-layouts  112 us (11%)
  blocking collectives  83.2 us (8%)
  between operations  25.6 us (2%)
    reduce_scatter x1, waiting for transfers between devices, on_device(): lax.psum_scatter(joined, ('dp', 'head'), scatter_dimension=0, tiled=True)  254 us
    reduce_scatter x1, waiting for transfers between devices, on_device(): rows_in = lax.psum_scatter(rows_out, 'dp', scatter_dimension=0, tiled=True)  156 us
    reduce_scatter x1, waiting for transfers between devices, on_device(): lax.psum_scatter(chosen_grads, ('dp', 'head'), scatter_dimension=0, tiled...  71.6 us
    dot_general x13, matrix products, contract_rows(): lax.dot_general(left, right, (((0,), (0,)), ((), ())), preferred_element_...  52.1 us
    all_gather x1, blocking collectives, on_device(): lax.all_gather(token_ids * 2 + valid, ('dp', 'head'), axis=1, tiled=True)  43.2 us
    psum x1, blocking collectives, on_device(): small = lax.psum(small, ('dp', 'head'))  39.9 us
    unnamed x336, local copies, waits for them, and re-layouts  30.1 us
    dot_general x13, matrix products, product(): return jnp.dot(left, right, preferred_element_type=jnp.float32)  29.4 us
  transfers between devices with their start and end apart: 12, of which 6 were waited for; matrix products, arithmetic and copies ran while one was open for 20% of the time, Pallas kernels for 0%

profile of v1, /device:TPU:0, one launch (start us, length us, event | category | flops | bytes accessed | tf_op | source)
XLA Modules:
  0.0 1017.6 jit_solution(17755199458363452493)
XLA Ops:
  8.8 43.2 %all_gather.21 = s32[2,4096]{1,0:T(2,128)S(1)} all-gather(s32[2,128]{1,0:T(2,128)S(1)} %multiply_add_fusion.2), channel_id=1, replica_groups=mesh['dp'=8,'head'=4] {'dp','head'}, dimensions={1}, use_global_device_ids=true | all-gather | bytes 33792 | tf_op jit(solution)/shard_map/all_gather | solution.py:216
  53.4 19.0 %gather_fusion = bf16[3072,768]{1,0:T(8,128)(2,1)} fusion(f32[4000,768]{1,0:T(8,128)} %param.25, s32[3072]{0:T(1024)S(1)} %broadcast_clamp_fusion), kind=kCustom, calls=%fused_computation | custom fusion | bytes 9449472 | tf_op jit(solution)/shard_map/gather | solution.py:230
  72.5 5.8 select_convert_fusion
  85.2 155.6 %reduce-scatter.4.cloned.1.call-done = bf16[1,384,768]{2,1,0:T(8,128)(2,1)} async-done(((bf16[8,384,768]{2,1,0:T(8,128)(2,1)}), bf16[1,384,768]{2,1,0:T(8,128)(2,1)}) %reduce-scatter.4.cloned.1.call-update) | async-done | bytes 589840 | tf_op jit(solution)/shard_map/reduce_scatter | solution.py:233
  242.5 24.4 %copy.52 = bf16[12288,768]{1,0:T(8,128)(2,1)} copy(bf16[12288,768]{0,1:T(8,128)(2,1)} %all-gather.10.cloned.1.call-done) | data formatting | bytes 37748736 | tf_op jit(solution)/shard_map/all_gather | solution.py:239
  283.5 8.4 slice.321
  292.0 4.9 slice.324
  342.7 5.2 multiply_reduce_fusion.10
  349.9 5.0 fusion.192
  373.3 4.6 convolution_bitcast_fusion.1
  386.2 4.7 convolution_convert_fusion
  432.4 71.6 %reduce-scatter.8.cloned.1.call-done = bf16[128,768]{1,0:T(8,128)(2,1)} async-done(((bf16[4096,768]{1,0:T(8,128)(2,1)}), bf16[128,768]{1,0:T(8,128)(2,1)}) %reduce-scatter.8.cloned.1.call-update) | async-done | bytes 196624 | tf_op jit(solution)/shard_map/reduce_scatter | solution.py:270
  509.8 8.3 fusion.50
  527.6 11.5 %add_convert_fusion = bf16[6144,768]{1,0:T(8,128)(2,1)} fusion(f32[6144,768]{1,0:T(8,128)} %fusion.50, bf16[256,3072]{1,0:T(8,128)(2,1)} %copy-done.90, bf16[256,3072]{1,0:T(8,128)(2,1)} %copy-done.89, f32[256,768]{1,0:T(8,128)S(1)} %copy-done.15, f32[768]{0:T(1024)S(1)} %get-tuple-element.64, f32[256]{0:T(256)S(1)} %copy-done.109), kind=kOutput, calls=%fused_computation.3 | convolution fusion | flops 2432237568 | bytes 32247808 | tf_op jit(solution)/shard_map/dot_general | solution.py:36
  539.1 6.8 add_convert_fusion.2
  545.9 15.0 %pad_maximum_fusion = bf16[32,384,768]{2,1,0:T(8,128)(2,1)} fusion(bf16[32,96,768]{2,1,0:T(8,128)(2,1)S(1)} %bitcast.267, bf16[32,192,768]{2,1,0:T(8,128)(2,1)} %bitcast.246, bf16[32,24,768]{2,1,0:T(8,128)(2,1)} %bitcast.273, bf16[32,72,768]{2,1,0:T(8,128)(2,1)} %bitcast.268), kind=kLoop, calls=%fused_computation.2 | loop fusion | flops 75497472 | bytes 37748736 | tf_op jit(solution)/shard_map/concatenate | solution.py:282
  561.7 23.2 %all-gather.8.cloned.1.call-done = bf16[3072,768]{1,0:T(8,128)(2,1)} async-done(((bf16[384,768]{1,0:T(8,128)(2,1)}), bf16[3072,768]{1,0:T(8,128)(2,1)}) %all-gather.8.cloned.1.call-update) | async-done | bytes 4718608 | tf_op jit(solution)/shard_map/all_gather | solution.py:288
  584.9 26.8 %scatter_custom_fusion = f32[4001,768]{1,0:T(8,128)} fusion(s32[3072]{0:T(1024)S(1)} %bitcast.299, bf16[3072,768]{1,0:T(8,128)(2,1)} %all-gather.8.cloned.1.call-done, f32[]{:T(128)} %constant.64.clone.1), kind=kCustom, calls=%fused_computation.13 | custom fusion | flops 4718592 | bytes 17009668 | tf_op jit(solution)/shard_map/scatter-add | solution.py:290
  611.7 7.7 slice.532
  627.4 254.2 %reduce-scatter.6.cloned.1.call-done = bf16[1,384,768]{2,1,0:T(8,128)(2,1)} async-done(((bf16[32,384,768]{2,1,0:T(8,128)(2,1)}), bf16[1,384,768]{2,1,0:T(8,128)(2,1)}) %reduce-scatter.6.cloned.1.call-update) | async-done | bytes 589840 | tf_op jit(solution)/shard_map/reduce_scatter | solution.py:285
  883.6 17.3 %reduce_sum.289 = bf16[4000,768]{1,0:T(8,128)(2,1)} reduce(bf16[4,4000,768]{2,1,0:T(8,128)(2,1)} %bitcast.265, bf16[]{:T(256)} %constant.84.clone.1), dimensions={0}, to_apply=%region_32.34 | reduce | flops 9216000 | bytes 30720002 | tf_op jit(solution)/shard_map/reduce_sum | solution.py:28
  900.9 6.6 fusion.2
  908.8 39.9 %all-reduce = (f32[2305]{0:T(1024)S(1)}, f32[]{:T(128)}) all-reduce(f32[2305]{0:T(1024)S(1)} %pad_maximum_fusion.18, f32[]{:T(128)S(6)} %add.363), channel_id=1, replica_groups=mesh['dp'=8,'head'=4] {'dp','head'}, use_global_device_ids=true, to_apply=%region_25.27 | all-reduce | flops 2306 | bytes 18448 | tf_op jit(solution)/shard_map/psum | solution.py:295
  978.0 28.9 %fusion.180 = (bf16[4000,768]{1,0:T(8,128)(2,1)}, f32[4000,768]{1,0:T(8,128)}, f32[4000,768]{1,0:T(8,128)}, f32[4000,768]{1,0:T(8,128)}) fusion(f32[4000,768]{1,0:T(8,128)} %param.25, f32[]{:T(128)S(6)} %div.137, bf16[4000,768]{1,0:T(8,128)(2,1)} %reduce_sum.289, f32[4000,768]{1,0:T(8,128)} %param.26, f32[4000,768]{1,0:T(8,128)} %param.27), kind=kLoop, calls=%fused_computation.347 | loop fusion | flops 55296000 | bytes 86016000 | tf_op jit(solution)/shard_map/convert_element_type | solution.py:347
  (527 shorter events, 193.1 us)
Async XLA Ops:
  8.0 72.6 %copy-start = (s32[2,1,3]{2,1,0:T(1,128)S(1)}, s32[2,1,3]{2,1,0:T(1,128)}, u32[]{:S(2)}) copy-start(s32[2,1,3]{2,1,0:T(1,128)} %param.17) | copy-start | bytes 76
  8.0 232.8 %reduce-scatter.4.cloned.1.call-start = ((), (), s32[]{:S(2)}) async-start(), calls=%async_computation.3 | async-start | bytes 5308416 | tf_op jit(solution)/shard_map/reduce_scatter | solution.py:233
  52.0 20.4 %copy-start.94 = (s32[2,4096]{1,0:T(2,128)}, s32[2,4096]{1,0:T(2,128)S(1)}, u32[]{:S(2)}) copy-start(s32[2,4096]{1,0:T(2,128)S(1)} %all_gather.21) | copy-start | bytes 98308
  78.4 164.2 %all-gather.10.cloned.1.call-start = ((), (), s32[]{:S(2)}) async-start(), calls=%async_computation.7 | async-start | bytes 19464192 | tf_op jit(solution)/shard_map/all_gather | solution.py:239
  80.5 269.4 %all-gather.12.cloned.1.call-start = ((), (), s32[]{:S(2)}) async-start(), calls=%async_computation.8 | async-start | bytes 6488064 | tf_op jit(solution)/shard_map/all_gather | solution.py:235
  83.1 183.9 %copy-start.135 = (s32[128]{0:T(128)}, s32[128]{0:T(128)S(1)}, u32[]{:S(2)}) copy-start(s32[128]{0:T(128)S(1)} %iota_add_fusion.3) | copy-start | bytes 1540
  269.3 48.1 %copy-start.4 = (bf16[32,72,768]{2,1,0:T(8,128)(2,1)}, bf16[32,72,768]{2,1,0:T(8,128)(2,1)S(1)}, u32[]{:S(2)}) copy-start(bf16[32,72,768]{2,1,0:T(8,128)(2,1)S(1)} %slice.311) | copy-start | bytes 10616836
  273.5 23.3 %collective-permute-start = (bf16[256,24,64]{0,2,1:T(8,128)(2,1)}, bf16[256,24,64]{0,2,1:T(8,128)(2,1)}, u32[]{:S(2)}, u32[]{:S(2)}) collective-permute-start(bf16[256,24,64]{0,2,1:T(8,128)(2,1)} %pad_maximum_fusion.12), channel_id=1, source_target_pairs={{0,1},{1,0},{2,3},{3,2},{4,5},{5,4},{6,7},{7,6},{8,9},{9,8},{10,11... | collective-permute-start | bytes 2359304 | tf_op jit(solution)/shard_map/ppermute | solution.py:112
  275.1 47.3 %collective-permute-start.2 = (bf16[128,4096]{1,0:T(8,128)(2,1)}, bf16[128,4096]{1,0:T(8,128)(2,1)}, u32[]{:S(2)}, u32[]{:S(2)}) collective-permute-start(bf16[128,4096]{1,0:T(8,128)(2,1)} %get-tuple-element.95), channel_id=1, source_target_pairs={{0,2},{1,3},{2,0},{3,1},{4,6},{5,7},{6,4},{7,5},{8,10},{9,11},{10,... | collective-permute-start | bytes 3145736 | tf_op jit(solution)/shard_map/ppermute | solution.py:112
  281.1 222.9 %reduce-scatter.8.cloned.1.call-start = ((), (), s32[]{:S(2)}) async-start(), calls=%async_computation.5 | async-start | bytes 6488064 | tf_op jit(solution)/shard_map/reduce_scatter | solution.py:270
  320.9 5.8 collective-permute-start.1
  337.2 31.7 %copy-start.16 = (f32[256,768]{1,0:T(8,128)}, f32[256,768]{1,0:T(8,128)S(1)}, u32[]{:S(2)}) copy-start(f32[256,768]{1,0:T(8,128)S(1)} %get-tuple-element.151) | copy-start | bytes 2359300
  384.2 6.8 collective-permute-start.3
  390.9 193.9 %all-gather.8.cloned.1.call-start = ((), (), s32[]{:S(2)}) async-start(), calls=%async_computation.6 | async-start | bytes 5308416 | tf_op jit(solution)/shard_map/all_gather | solution.py:288
  422.6 2.4 collective-permute-start.4
  432.1 74.0 %copy-start.26 = (f32[256,768]{1,0:T(8,128)S(1)}, f32[256,768]{1,0:T(8,128)}, u32[]{:S(2)}) copy-start(f32[256,768]{1,0:T(8,128)} %copy-done.24) | copy-start | bytes 2359300
  432.4 75.3 %copy-start.34 = (bf16[256,3072]{1,0:T(8,128)(2,1)S(1)}, bf16[256,3072]{1,0:T(8,128)(2,1)}, u32[]{:S(2)}) copy-start(bf16[256,3072]{1,0:T(8,128)(2,1)} %copy-done.33) | copy-start | bytes 4718596
  505.8 375.8 %reduce-scatter.6.cloned.1.call-start = ((), (), s32[]{:S(2)}) async-start(), calls=%async_computation.4 | async-start | bytes 19464192 | tf_op jit(solution)/shard_map/reduce_scatter | solution.py:285
  560.9 322.6 %all-gather.14.cloned.1.call-start = ((), (), s32[]{:S(2)}) async-start(), calls=%async_computation.9 | async-start | bytes 30720000 | tf_op jit(solution)/shard_map/all_gather | solution.py:27
  900.9 62.1 %slice-start.16 = ((s8[9437184]{0:T(1024)(128)(4,1)}), s8[1048576]{0:T(1024)(128)(4,1)S(1)}, s32[]{:S(2)}) async-start(s8[9437184]{0:T(1024)(128)(4,1)} %bitcast.255), calls=%async_computation.26 | async-start | bytes 2097152
  978.0 28.9 %copy-start.106 = (f32[3,768]{1,0:T(4,128)S(1)}, f32[3,768]{1,0:T(4,128)}, u32[]{:S(2)}) copy-start(f32[3,768]{1,0:T(4,128)} %param.28) | copy-start | bytes 27652
  978.0 28.9 %copy-start.116 = (f32[3,768]{1,0:T(4,128)S(1)}, f32[3,768]{1,0:T(4,128)}, u32[]{:S(2)}) copy-start(f32[3,768]{1,0:T(4,128)} %param.29) | copy-start | bytes 27652
  978.0 28.9 %copy-start.117 = (f32[3,768]{1,0:T(4,128)S(1)}, f32[3,768]{1,0:T(4,128)}, u32[]{:S(2)}) copy-start(f32[3,768]{1,0:T(4,128)} %param.30) | copy-start | bytes 27652
  978.0 29.6 %copy-start.1 = (s32[2,1,3]{2,1,0:T(1,128)S(1)}, s32[2,1,3]{2,1,0:T(1,128)}, u32[]{:S(2)}) copy-start(s32[2,1,3]{2,1,0:T(1,128)} %param.17) | copy-start | bytes 76
  (153 other events, 634.0 us)
Sparse Core Ops, SparseCore 0:
  78.5 162.2 reduce-scatter.3
  505.9 78.8 all-gather.7
  619.6 150.5 all-gather.13
Sparse Core Ops, SparseCore 1:
  82.3 157.9 all-gather.9
  281.2 68.7 all-gather.11
  391.0 113.0 reduce-scatter.7
  561.0 320.5 reduce-scatter.5
